TPU v7x, 128 devices: a whole 4x4x4 slice. The times are simulated.
128 devices in a mesh: dp: 16 (over z, x_hi, core), tensor: 8 (over y, x_lo).
Axes of the slice: x: 4 (x_hi: 2, x_lo: 2; x = x_hi * 2 + x_lo), y: 4, z: 4, core: 2. Of those that a mesh axis runs over, the one named last changes fastest.
Arguments:
- tokens: bfloat16 [16384, 5120], P(('dp', 'tensor')), may hold values from -6 to 6
- lengths: int32 [16], P('dp'), may hold values from 128 to 1024, as said below
- attn_gain: float32 [5120], replicated, may hold values from 0.5 to 1.5
- q_gain: float32 [128], replicated, may hold values from 0.8 to 20
- key_norm_gain: float32 [128], replicated, may hold values from 0.8 to 20
- wq_param: float32 [5120, 8192], P('dp', 'tensor'), may hold values from -0.078125 to 0.078125
- wq_moment: float32 [5120, 8192], P('dp', 'tensor'), may hold values from -4 to 4
- wq_second: float32 [5120, 8192], P('dp', 'tensor'), may hold values from 0.01 to 4
- wq_grad: float32 [5120, 8192], P('dp', 'tensor'), may hold values from -6 to 6
- key_weight_matrix: float32 [5120, 1024], P('dp', 'tensor'), may hold values from -0.078125 to 0.078125
- key_weight_first_moment: float32 [5120, 1024], P('dp', 'tensor'), may hold values from -4 to 4
- key_weight_second_moment: float32 [5120, 1024], P('dp', 'tensor'), may hold values from 0.01 to 4
- key_weight_gradient: float32 [5120, 1024], P('dp', 'tensor'), may hold values from -6 to 6
- value_weight_matrix: float32 [5120, 1024], P('dp', 'tensor'), may hold values from -0.078125 to 0.078125
- value_weight_first_moment: float32 [5120, 1024], P('dp', 'tensor'), may hold values from -4 to 4
- value_weight_second_moment: float32 [5120, 1024], P('dp', 'tensor'), may hold values from 0.01 to 4
- value_weight_gradient: float32 [5120, 1024], P('dp', 'tensor'), may hold values from -6 to 6
- wo_param: float32 [5120, 8192], P('dp', 'tensor'), may hold values from -0.0625 to 0.0625
- wo_moment: float32 [5120, 8192], P('dp', 'tensor'), may hold values from -4 to 4
- wo_second: float32 [5120, 8192], P('dp', 'tensor'), may hold values from 0.01 to 4
- wo_grad: float32 [5120, 8192], P('dp', 'tensor'), may hold values from -6 to 6
Outputs:
- attended: bfloat16 [16384, 5120], P(('dp', 'tensor'))
- wq_param_new: float32 [5120, 8192], P('dp', 'tensor')
- wq_moment_new: float32 [5120, 8192], P('dp', 'tensor')
- wq_second_new: float32 [5120, 8192], P('dp', 'tensor')
- wk_param_new: float32 [5120, 1024], P('dp', 'tensor')
- wk_moment_new: float32 [5120, 1024], P('dp', 'tensor')
- wk_second_new: float32 [5120, 1024], P('dp', 'tensor')
- wv_param_new: float32 [5120, 1024], P('dp', 'tensor')
- wv_moment_new: float32 [5120, 1024], P('dp', 'tensor')
- wv_second_new: float32 [5120, 1024], P('dp', 'tensor')
- wo_param_new: float32 [5120, 8192], P('dp', 'tensor')
- wo_moment_new: float32 [5120, 8192], P('dp', 'tensor')
- wo_second_new: float32 [5120, 8192], P('dp', 'tensor')
Inputs may be any that keep to these rules, and one draw needn't show every extreme that they name: Positions of prompt p at or past lengths[p] are padding; in every draw some prompt is full.
All inputs are finite; a program needn't handle non-finite values.
Results may differ from a plain program's by a relative error of at most 0.019.
The roundings to bfloat16 on the way count: a program that leaves them out, or rounds other values in their place, can miss the bound.
Values may be sent and summed in bfloat16 or wider, within the bound.
No kernel may reach another device: no remote copies, remote signals or barrier semaphores. Data moves between devices by JAX's collectives and lax.ppermute only.
A program may use at most 192 MiB of HBM per device.

v0:
```python
import math

import jax
import jax.numpy as jnp
from jax import lax
from jax.sharding import PartitionSpec as P

HEAD_SIZE = 128
STEP = 10


BETA_ONE = 0.9
BETA_TWO = 0.999
ADAM_EPS = 1e-08
LEARN_RATE = 0.0001
DECAY_RATE = 0.01
NORM_EPS = 1e-06
ROPE_BASE = 1000000.0


def adamw_step(current, moment, second, gradient):
    moment_new = BETA_ONE * moment + (1.0 - BETA_ONE) * gradient
    second_new = BETA_TWO * second + (1.0 - BETA_TWO) * gradient * gradient
    moment_hat = moment_new / (1.0 - BETA_ONE**STEP)
    second_hat = second_new / (1.0 - BETA_TWO**STEP)
    updated = current - LEARN_RATE * (
        moment_hat / (jnp.sqrt(second_hat) + ADAM_EPS) + DECAY_RATE * current
    )
    return (updated, moment_new, second_new)


def root_mean_scale(values, gain):
    mean_sq = jnp.mean(values * values, axis=-1, keepdims=True)
    return values * lax.rsqrt(mean_sq + NORM_EPS) * gain


def rope_tables(count, width):
    places = jnp.arange(count, dtype=jnp.float32)
    freqs = ROPE_BASE ** (-jnp.arange(0, width, 2, dtype=jnp.float32) / width)
    angles = places[:, None] * freqs[None, :]
    angles = jnp.concatenate([angles, angles], axis=-1)
    return (jnp.cos(angles), jnp.sin(angles))


def rotate_positions(values, cosine_table, sine_values):
    half = values.shape[-1] // 2
    turned = jnp.concatenate([-values[..., half:], values[..., :half]], axis=-1)
    return values * cosine_table[:, None, :] + turned * sine_values[:, None, :]


def attend(query_rows, key_row_block, value_row_block, length):
    count = query_rows.shape[0]
    heads = query_rows.shape[1]
    groups = key_row_block.shape[1]
    share = heads // groups
    grouped = query_rows.reshape(count, groups, share, HEAD_SIZE).transpose(1, 2, 0, 3)
    keys_first = key_row_block.transpose(1, 0, 2)
    values_first = value_row_block.transpose(1, 0, 2)
    places = jnp.arange(count, dtype=jnp.int32)
    visible = (places[None, :] <= places[:, None]) & (places[None, :] < length)

    def one_group(items):
        q_block, k_block, v_block = items
        scores = jnp.einsum(
            "gsd,td->gst", q_block, k_block, preferred_element_type=jnp.float32
        ) / math.sqrt(HEAD_SIZE)
        masked = jnp.where(visible[None], scores, -1e30)
        maxima = jnp.max(masked, axis=-1, keepdims=True)
        exps = jnp.where(visible[None], jnp.exp(masked - maxima), 0.0)
        totals = jnp.sum(exps, axis=-1, keepdims=True)
        probs = (exps / totals).astype(jnp.bfloat16)
        mixed = jnp.einsum("gst,td->gsd", probs, v_block, preferred_element_type=jnp.float32)
        return mixed.astype(jnp.bfloat16)

    context = lax.map(one_group, (grouped, keys_first, values_first))
    return context.transpose(2, 0, 1, 3).reshape(count, heads * HEAD_SIZE)


def local(
    tokens,
    lengths,
    attn_gain,
    q_gain,
    key_norm_gain,
    wq_param,
    wq_moment,
    wq_second,
    wq_grad,
    key_weight_matrix,
    key_weight_first_moment,
    key_weight_second_moment,
    key_weight_gradient,
    value_weight_matrix,
    value_weight_first_moment,
    value_weight_second_moment,
    value_weight_gradient,
    wo_param,
    wo_moment,
    wo_second,
    wo_grad,
):
    new_q = adamw_step(wq_param, wq_moment, wq_second, wq_grad)
    new_k = adamw_step(
        key_weight_matrix, key_weight_first_moment, key_weight_second_moment, key_weight_gradient
    )
    new_v = adamw_step(
        value_weight_matrix,
        value_weight_first_moment,
        value_weight_second_moment,
        value_weight_gradient,
    )
    new_o = adamw_step(wo_param, wo_moment, wo_second, wo_grad)
    shard_q = new_q[0].astype(jnp.bfloat16)
    shard_k = new_k[0].astype(jnp.bfloat16)
    shard_v = new_v[0].astype(jnp.bfloat16)
    shard_o = new_o[0].astype(jnp.bfloat16)
    normed_own = root_mean_scale(tokens.astype(jnp.float32), attn_gain).astype(jnp.bfloat16)
    normed = lax.all_gather(normed_own, "tensor", axis=0, tiled=True)
    count = normed.shape[0]
    whole_q, whole_k, whole_v, whole_o = (
        lax.all_gather(shard_q, "dp", axis=0, tiled=True),
        lax.all_gather(shard_k, "dp", axis=0, tiled=True),
        lax.all_gather(shard_v, "dp", axis=0, tiled=True),
        lax.all_gather(shard_o, "dp", axis=0, tiled=True),
    )
    query_flat = jnp.dot(normed, whole_q, preferred_element_type=jnp.float32)
    key_flattened = jnp.dot(normed, whole_k, preferred_element_type=jnp.float32)
    value_flattened = jnp.dot(normed, whole_v, preferred_element_type=jnp.float32)
    cosine_table, sine_values = rope_tables(count, HEAD_SIZE)
    query_rows = rotate_positions(
        root_mean_scale(query_flat.reshape(count, -1, HEAD_SIZE), q_gain), cosine_table, sine_values
    ).astype(jnp.bfloat16)
    key_row_block = rotate_positions(
        root_mean_scale(key_flattened.reshape(count, -1, HEAD_SIZE), key_norm_gain),
        cosine_table,
        sine_values,
    ).astype(jnp.bfloat16)
    value_row_block = value_flattened.astype(jnp.bfloat16).reshape(count, -1, HEAD_SIZE)
    context = attend(query_rows, key_row_block, value_row_block, lengths[0])
    partial_value = lax.dot_general(
        context, whole_o, (((1,), (1,)), ((), ())), preferred_element_type=jnp.float32
    )
    rounded = partial_value.astype(jnp.bfloat16)
    attended = (
        lax.psum_scatter(rounded, "tensor", scatter_dimension=0, tiled=True)
        .astype(jnp.float32)
        .astype(jnp.bfloat16)
    )
    return (
        attended,
        new_q[0],
        new_q[1],
        new_q[2],
        new_k[0],
        new_k[1],
        new_k[2],
        new_v[0],
        new_v[1],
        new_v[2],
        new_o[0],
        new_o[1],
        new_o[2],
    )


def solution(mesh):
    placed = (
        P(("dp", "tensor"), None),
        P("dp"),
        P(),
        P(),
        P(),
        P("dp", "tensor"),
        P("dp", "tensor"),
        P("dp", "tensor"),
        P("dp", "tensor"),
        P("dp", "tensor"),
        P("dp", "tensor"),
        P("dp", "tensor"),
        P("dp", "tensor"),
        P("dp", "tensor"),
        P("dp", "tensor"),
        P("dp", "tensor"),
        P("dp", "tensor"),
        P("dp", "tensor"),
        P("dp", "tensor"),
        P("dp", "tensor"),
        P("dp", "tensor"),
    )
    return jax.shard_map(
        local,
        mesh=mesh,
        in_specs=placed,
        out_specs=(
            P(("dp", "tensor"), None),
            P("dp", "tensor"),
            P("dp", "tensor"),
            P("dp", "tensor"),
            P("dp", "tensor"),
            P("dp", "tensor"),
            P("dp", "tensor"),
            P("dp", "tensor"),
            P("dp", "tensor"),
            P("dp", "tensor"),
            P("dp", "tensor"),
            P("dp", "tensor"),
            P("dp", "tensor"),
        ),
        check_vma=False,
    )
```

profile of v0, /device:TPU:1, one launch (start us, length us, event | category | flops | bytes accessed | tf_op | source)
XLA Modules:
  0.0 713.0 jit_solution(2683456082950338982)
XLA Ops:
  7.2 0.0 all-gather.10.cloned.1.call-start
  7.2 2.6 fusion.33
  9.8 0.0 all-gather.6.cloned.1.call-start
  9.9 0.3 fusion.12
  10.3 1.4 fusion.14
  11.7 0.0 all-gather.8.cloned.1.call-start
  11.8 5.2 fusion.37
  17.0 0.0 all-gather.12.cloned.1.call-start
  17.0 0.5 all-gather.12.cloned.1.call-update
  17.6 0.0 all-gather.14.cloned.1.call-start
  17.6 5.1 fusion.31
  22.8 0.2 reduce-scatter.2.cloned.1.call-start
  23.7 0.1 iota_multiply_fusion
  23.8 0.4 fusion.9
  24.1 35.6 %all-gather.10.cloned.1.call-done = bf16[5120,128]{1,0:T(8,128)(2,1)} async-done(((bf16[320,128]{1,0:T(8,128)(2,1)}), bf16[5120,128]{1,0:T(8,128)(2,1)}) %all-gather.10.cloned.1.call-update) | async-done | bytes 1310736 | tf_op jit(solution)/shard_map/all_gather | solution.py:122
  59.8 208.2 %all-gather.6.cloned.1.call-done = bf16[1024,5120]{1,0:T(8,128)(2,1)} async-done(((bf16[128,5120]{1,0:T(8,128)(2,1)}), bf16[1024,5120]{1,0:T(8,128)(2,1)}) %all-gather.6.cloned.1.call-update) | async-done | bytes 10485776 | tf_op jit(solution)/shard_map/all_gather | solution.py:118
  268.0 7.9 %multiply_reduce_fusion.1 = (f32[1024]{0:T(1024)S(1)}, f32[1024,128]{0,1:T(8,128)S(1)}) fusion(bf16[1024,5120]{1,0:T(8,128)(2,1)} %all-gather.6.cloned.1.call-done, bf16[5120,128]{1,0:T(8,128)(2,1)} %all-gather.10.cloned.1.call-done), kind=kOutput, calls=%fused_computation.45 | convolution fusion | flops 1342438400 | bytes 12324864 | tf_op jit(solution)/shard_map/dot_general | solution.py:127
  275.9 0.1 fusion.24
  276.1 2.2 fusion.25
  278.2 0.2 copy.35
  278.4 0.2 copy.37
  278.6 75.3 %all-gather.8.cloned.1.call-done = bf16[5120,1024]{1,0:T(8,128)(2,1)} async-done(((bf16[320,1024]{1,0:T(8,128)(2,1)}), bf16[5120,1024]{1,0:T(8,128)(2,1)}) %all-gather.8.cloned.1.call-update) | async-done | bytes 10485776 | tf_op jit(solution)/shard_map/all_gather | solution.py:121
  353.9 18.1 %multiply_reduce_fusion = (f32[1024,8]{0,1:T(8,128)S(1)}, f32[1024,1024]{0,1:T(8,128)}) fusion(bf16[1024,5120]{1,0:T(8,128)(2,1)} %all-gather.6.cloned.1.call-done, bf16[5120,1024]{1,0:T(8,128)(2,1)} %all-gather.8.cloned.1.call-done), kind=kOutput, calls=%fused_computation.17 | convolution fusion | flops 10739507200 | bytes 25198592 | tf_op jit(solution)/shard_map/dot_general | solution.py:126
  372.1 5.3 copy.36
  377.4 5.4 copy.34
  382.8 3.8 multiply_multiply_fusion
  386.6 4.6 fusion.6
  391.3 21.3 %fusion.39 = (f32[8,1024]{1,0:T(8,128)S(1)}, f32[8,1024,1024]{1,2,0:T(8,128)}) fusion(pred[1024,1024]{0,1:T(8,128)(4,1)S(1)} %fusion.9, bf16[1024,128,1]{0,1,2:T(8,128)(2,1)S(1)} %get-tuple-element.51, f32[1024,1,8,64]{3,0,2,1:T(8,128)} %get-tuple-element.48, f32[1024,1,8,64]{3,0,2,1:T(8,128)} %get-tuple-element.47, f32[1024,1,8,128]{3,0,2,1:T(8,128)} %copy.34, ...), kind=kOutput, calls=%fused_computation.71 | convolution fusion | flops 2196767744 | bytes 44368384 | tf_op jit(solution)/shard_map/while/body/eval_jaxpr/sub | solution.py:69
  412.6 23.5 %fusion.16 = bf16[8,1024,128]{1,2,0:T(8,128)(2,1)S(1)} fusion(f32[8,1024,1024]{1,2,0:T(8,128)} %get-tuple-element.59, f32[8,1024]{1,0:T(8,128)S(1)} %get-tuple-element.58, bf16[1024,5120]{1,0:T(8,128)(2,1)} %all-gather.6.cloned.1.call-done, bf16[5120,128]{1,0:T(8,128)(2,1)} %all-gather.12.cloned.1.call-done), kind=kOutput, calls=%fused_computation.29 | convolution fusion | flops 3507617792 | bytes 47480832 | tf_op jit(solution)/shard_map/while/body/eval_jaxpr/gst,td->gsd/dot_general | solution.py:72
  436.1 46.6 %all-gather.14.cloned.1.call-done = bf16[5120,1024]{1,0:T(8,128)(2,1)} async-done(((bf16[320,1024]{1,0:T(8,128)(2,1)}), bf16[5120,1024]{1,0:T(8,128)(2,1)}) %all-gather.14.cloned.1.call-update) | async-done | bytes 10485776 | tf_op jit(solution)/shard_map/all_gather | solution.py:124
  482.7 17.4 %convolution_convert_fusion = bf16[1024,5120]{1,0:T(8,128)(2,1)} fusion(bf16[1024,1024]{0,1:T(8,128)(2,1)S(1)} %bitcast.45, bf16[5120,1024]{1,0:T(8,128)(2,1)} %all-gather.14.cloned.1.call-done), kind=kOutput, calls=%fused_computation.9 | convolution fusion | flops 10742661120 | bytes 23068672 | tf_op jit(solution)/shard_map/dot_general | solution.py:140
  500.1 206.1 %reduce-scatter.2.cloned.1.call-done = bf16[128,5120]{1,0:T(8,128)(2,1)} async-done(((bf16[1024,5120]{1,0:T(8,128)(2,1)}), bf16[128,5120]{1,0:T(8,128)(2,1)}) %reduce-scatter.2.cloned.1.call-update) | async-done | bytes 1310736 | tf_op jit(solution)/shard_map/reduce_scatter | solution.py:145
  (24 shorter events, 0.2 us)
Async XLA Ops:
  7.2 2.7 copy-start
  7.2 3.1 copy-start.3
  7.2 52.6 %all-gather.10.cloned.1.call-start = ((), (), s32[]{:S(2)}) async-start(), calls=%async_computation.3 | async-start | bytes 1392640 | tf_op jit(solution)/shard_map/all_gather | solution.py:122
  9.8 258.1 %all-gather.6.cloned.1.call-start = ((), (), s32[]{:S(2)}) async-start(), calls=%async_computation.1 | async-start | bytes 11796480 | tf_op jit(solution)/shard_map/all_gather | solution.py:118
  10.2 1.6 copy-start.1
  11.7 5.9 copy-start.2
  11.7 342.2 %all-gather.8.cloned.1.call-start = ((), (), s32[]{:S(2)}) async-start(), calls=%async_computation.2 | async-start | bytes 11141120 | tf_op jit(solution)/shard_map/all_gather | solution.py:121
  17.0 395.6 %all-gather.12.cloned.1.call-start = ((), (), s32[]{:S(2)}) async-start(), calls=%async_computation.4 | async-start | bytes 1392640 | tf_op jit(solution)/shard_map/all_gather | solution.py:123
  17.6 465.1 %all-gather.14.cloned.1.call-start = ((), (), s32[]{:S(2)}) async-start(), calls=%async_computation.5 | async-start | bytes 11141120 | tf_op jit(solution)/shard_map/all_gather | solution.py:124
  22.8 683.4 %reduce-scatter.2.cloned.1.call-start = ((), (), s32[]{:S(2)}) async-start(), calls=%async_computation.6 | async-start | bytes 11796480 | tf_op jit(solution)/shard_map/reduce_scatter | solution.py:145
  24.1 251.8 %copy-start.4 = (f32[128]{0:T(128)S(1)}, f32[128]{0:T(128)}, u32[]{:S(2)}) copy-start(f32[128]{0:T(128)} %param.25) | copy-start | bytes 1540
  377.4 5.4 copy-start.5
Sparse Core Ops, SparseCore 0:
  10.5 49.2 all-gather.9
  62.0 205.9 all-gather.5
  270.4 83.4 all-gather.7
  356.3 43.2 all-gather.11
  401.9 80.7 all-gather.13
  500.2 205.8 reduce-scatter.1
where the time goes:
time: 713 us
  waiting for transfers between devices  572 us (80%)
  matrix products  88.3 us (12%)
  other arithmetic  25.9 us (4%)
  between operations  15 us (2%)
  local copies, waits for them, and re-layouts  11.1 us (2%)
    all_gather x1, waiting for transfers between devices, local(): normed = lax.all_gather(normed_own, 'tensor', axis=0, tiled=True)  208 us
    reduce_scatter x1, waiting for transfers between devices, local(): lax.psum_scatter(rounded, 'tensor', scatter_dimension=0, tiled=True)  206 us
    all_gather x1, waiting for transfers between devices, local(): lax.all_gather(shard_q, 'dp', axis=0, tiled=True)  75.3 us
    all_gather x1, waiting for transfers between devices, local(): lax.all_gather(shard_o, 'dp', axis=0, tiled=True)  46.6 us
    all_gather x1, waiting for transfers between devices, local(): lax.all_gather(shard_k, 'dp', axis=0, tiled=True)  35.6 us
    dot_general x1, matrix products, one_group(): jnp.einsum('gst,td->gsd', probs, v_block, preferred_element_type=jnp.floa...  23.5 us
    sub x1, matrix products, one_group(): exps = jnp.where(visible[None], jnp.exp(masked - maxima), 0.0)  21.3 us
    dot_general x1, matrix products, local(): query_flat = jnp.dot(normed, whole_q, preferred_element_type=jnp.float32)  18.1 us
  transfers between devices with their start and end apart: 6, of which 5 were waited for; matrix products, arithmetic and copies ran while one was open for 15% of the time, Pallas kernels for 0%

commit v1 on v0

v1 whole, which is shorter than its diff:
```python
import functools
import itertools
import math

import jax
import jax.numpy as jnp
from jax import lax
from jax.experimental import pallas as pl
from jax.experimental.pallas import tpu as pltpu
from jax.sharding import Mesh
from jax.sharding import PartitionSpec as P

HEAD_SIZE = 128
STEP = 10

BETA_ONE = 0.9
BETA_TWO = 0.999
ADAM_EPS = 1e-08
LEARN_RATE = 0.0001
DECAY_RATE = 0.01
NORM_EPS = 1e-06
ROPE_BASE = 1000000.0

AXES = ("z", "xh", "c", "y", "xl")
SIZES = dict(z=4, xh=2, c=2, y=4, xl=2)
WIDTH = 5120
BLOCK = 128
OWN = 512
BF16 = jnp.bfloat16
F32 = jnp.float32


def adamw_step(current, moment, second, gradient):
    moment_new = BETA_ONE * moment + (1.0 - BETA_ONE) * gradient
    second_new = BETA_TWO * second + (1.0 - BETA_TWO) * gradient * gradient
    moment_hat = moment_new / (1.0 - BETA_ONE**STEP)
    second_hat = second_new / (1.0 - BETA_TWO**STEP)
    updated = current - LEARN_RATE * (
        moment_hat / (jnp.sqrt(second_hat) + ADAM_EPS) + DECAY_RATE * current
    )
    return (updated, moment_new, second_new)


def root_mean_scale(values, gain):
    mean_sq = jnp.mean(values * values, axis=-1, keepdims=True)
    return values * lax.rsqrt(mean_sq + NORM_EPS) * gain


def permute(axes, move):
    axes = tuple(a for a in AXES if a in axes)
    places = list(itertools.product(*[range(SIZES[a]) for a in axes]))
    index = {place: i for i, place in enumerate(places)}
    pairs = []
    for place in places:
        there = move(dict(zip(axes, place)))
        pairs.append((index[place], index[tuple(there[a] for a in axes)]))
    return lambda v: lax.ppermute(v, axes, pairs)


def ring_move(axis):
    def move(place):
        step = 1 if place["c"] == 0 else -1
        if axis == "x":
            x = (place["xh"] * 2 + place["xl"] + step) % 4
            place["xh"], place["xl"] = x // 2, x % 2
        else:
            place[axis] = (place[axis] + step) % SIZES[axis]
        return place

    return move


def swap_move(axis):
    def move(place):
        place[axis] = 1 - place[axis]
        return place

    return move


ring_y = permute(("y", "c"), ring_move("y"))
swap_xl = permute(("xl",), swap_move("xl"))


def position_tables(xl):
    block = jnp.arange(4, dtype=jnp.int32)[:, None] * 2 + xl
    places = (block * BLOCK + jnp.arange(BLOCK, dtype=jnp.int32)[None, :]).reshape(-1)
    freqs = ROPE_BASE ** (-jnp.arange(0, HEAD_SIZE, 2, dtype=F32) / HEAD_SIZE)
    angles = places.astype(F32)[:, None] * freqs[None, :]
    cosine, sine = jnp.cos(angles), jnp.sin(angles)
    return (
        jnp.concatenate([cosine, cosine], axis=-1),
        jnp.concatenate([-sine, sine], axis=-1),
    )


def norm_rope(u, gain, cosine, sine):
    mean_sq = jnp.mean(u * u, axis=-1, keepdims=True)
    u = u * lax.rsqrt(mean_sq + NORM_EPS) * gain
    return u * cosine + pltpu.roll(u, HEAD_SIZE // 2, 1) * sine


def qkv_kernel(x_ref, w_ref, cos_ref, sin_ref, qg_ref, kg_ref, q_ref, kv_ref, acc):
    step = pl.program_id(1)
    last = pl.num_programs(1) - 1
    rows = x_ref[...]
    for n in range(0, 1280, 256):
        part = w_ref[0, :, 0, :, :, n : n + 256].reshape(1280, 256)
        out = jnp.dot(rows, part, preferred_element_type=F32)

        @pl.when(step == 0)
        def _():
            acc[:, n : n + 256] = out

        @pl.when(step > 0)
        def _():
            acc[:, n : n + 256] += out

    @pl.when(step == last)
    def _():
        cosine, sine = cos_ref[...], sin_ref[...]
        for h in range(8):
            u = acc[:, h * 128 : (h + 1) * 128]
            q_ref[0, :, h * 128 : (h + 1) * 128] = norm_rope(u, qg_ref[...], cosine, sine).astype(BF16)
        kv_ref[0, :, :128] = norm_rope(acc[:, 1024:1152], kg_ref[...], cosine, sine).astype(BF16)
        kv_ref[0, :, 128:] = acc[:, 1152:1280].astype(BF16)


def qkv_project(rows, weights, cosine, sine, q_gain, k_gain):
    whole = lambda shape: pl.BlockSpec(shape, lambda g, s: (0,) * len(shape))
    return pl.pallas_call(
        qkv_kernel,
        grid=(2, 4),
        in_specs=[
            pl.BlockSpec((OWN, 1280), lambda g, s: (0, s)),
            pl.BlockSpec((1, 2, 1, 2, 320, 1280), lambda g, s: (s, 0, g, 0, 0, 0)),
            whole((OWN, 128)),
            whole((OWN, 128)),
            whole((1, 128)),
            whole((1, 128)),
        ],
        out_specs=[
            pl.BlockSpec((1, OWN, 1024), lambda g, s: (g, 0, 0)),
            pl.BlockSpec((1, OWN, 256), lambda g, s: (g, 0, 0)),
        ],
        out_shape=[
            jax.ShapeDtypeStruct((2, OWN, 1024), BF16),
            jax.ShapeDtypeStruct((2, OWN, 256), BF16),
        ],
        scratch_shapes=[pltpu.VMEM((OWN, 1280), F32)],
        compiler_params=pltpu.CompilerParams(vmem_limit_bytes=48 << 20),
        cost_estimate=pl.CostEstimate(flops=2 * 512 * 5120 * 2560, bytes_accessed=40 << 20, transcendentals=0),
        name="qkv",
    )(rows, weights, cosine, sine, q_gain, k_gain)


SCALE = math.log2(math.e) / math.sqrt(HEAD_SIZE)


def attend_kernel(info_ref, q_ref, own_ref, far_ref, o_ref):
    length, xl = info_ref[0], info_ref[1]
    block = pl.program_id(1)

    def body(j):
        n = (j + 1) * BLOCK
        keys = jnp.concatenate([own_ref[0, :n, :128], far_ref[0, :n, :128]], axis=0)
        values = jnp.concatenate([own_ref[0, :n, 128:], far_ref[0, :n, 128:]], axis=0)
        row = lax.broadcasted_iota(jnp.int32, (BLOCK, 2 * n), 0)
        col = lax.broadcasted_iota(jnp.int32, (BLOCK, 2 * n), 1)
        own = col < n
        inner = jnp.where(own, col, col - n)
        side = jnp.where(own, xl, 1 - xl)
        place = (inner // BLOCK * 2 + side) * BLOCK + inner % BLOCK
        query = (2 * j + xl) * BLOCK + row
        bias = jnp.where((place <= query) & (place < length), 0.0, -1e30).astype(F32)
        for h in range(8):
            lanes = slice(h * 128, (h + 1) * 128)
            scores = lax.dot_general(
                q_ref[0, :, lanes], keys, (((1,), (1,)), ((), ())), preferred_element_type=F32
            )
            scores = scores + bias
            top = jnp.max(scores, axis=-1, keepdims=True)
            exps = jnp.exp2((scores - top) * SCALE)
            total = jnp.sum(exps, axis=-1, keepdims=True)
            mixed = jnp.dot(exps.astype(BF16), values, preferred_element_type=F32)
            o_ref[0, :, lanes] = (mixed / total).astype(BF16)

    for j in range(4):
        pl.when(block == j)(functools.partial(body, j))


def attend(info, queries, own, far):
    return pl.pallas_call(
        attend_kernel,
        grid=(2, 4),
        in_specs=[
            pl.BlockSpec(memory_space=pltpu.SMEM),
            pl.BlockSpec((1, BLOCK, 1024), lambda g, j: (g, j, 0)),
            pl.BlockSpec((1, OWN, 256), lambda g, j: (g, 0, 0)),
            pl.BlockSpec((1, OWN, 256), lambda g, j: (g, 0, 0)),
        ],
        out_specs=pl.BlockSpec((1, BLOCK, 1024), lambda g, j: (g, j, 0)),
        out_shape=jax.ShapeDtypeStruct((2, OWN, 1024), BF16),
        compiler_params=pltpu.CompilerParams(vmem_limit_bytes=48 << 20),
        cost_estimate=pl.CostEstimate(flops=6 << 30, bytes_accessed=5 << 20, transcendentals=5 << 20),
        name="attend",
    )(info, queries, own, far)


def out_kernel(ctx_ref, w_ref, o_ref):
    for f in range(4):
        total = None
        for g in range(2):
            part = lax.dot_general(
                ctx_ref[g],
                w_ref[0, f // 2, g, f % 2],
                (((1,), (1,)), ((), ())),
                preferred_element_type=F32,
            )
            total = part if total is None else total + part
        o_ref[:, f * 320 : (f + 1) * 320] = total.astype(BF16)


def out_project(context, weights, first, count):
    return pl.pallas_call(
        out_kernel,
        grid=(count,),
        in_specs=[
            pl.BlockSpec((2, OWN, 1024), lambda s: (0, 0, 0)),
            pl.BlockSpec((1, 2, 2, 2, 320, 1024), lambda s: (s + first, 0, 0, 0, 0, 0)),
        ],
        out_specs=pl.BlockSpec((OWN, 1280), lambda s: (0, s)),
        out_shape=jax.ShapeDtypeStruct((OWN, 1280 * count), BF16),
        compiler_params=pltpu.CompilerParams(vmem_limit_bytes=48 << 20),
        cost_estimate=pl.CostEstimate(
            flops=2 * 512 * 2048 * 1280 * count, bytes_accessed=count * (7 << 20), transcendentals=0
        ),
        name="out_project",
    )(context, weights)


def scatter_sum(partial, y, core):
    blocks = partial.reshape(4, BLOCK, -1)
    step = 1 - 2 * core

    def own(back):
        return lax.dynamic_index_in_dim(blocks, jnp.mod(y - step * back, 4), 0, keepdims=False)

    moving = own(1)
    for s in range(1, 4):
        arrived = ring_y(moving)
        moving = (arrived.astype(F32) + own(s + 1).astype(F32)).astype(BF16)
    return moving


def gather_tokens(mine, y, core):
    step = 1 - 2 * core
    whole = jnp.zeros((4, BLOCK, WIDTH), BF16)
    moving = mine
    for s in range(4):
        whole = lax.dynamic_update_index_in_dim(whole, moving, jnp.mod(y - step * s, 4), 0)
        if s < 3:
            moving = ring_y(moving)
    return whole.reshape(OWN, WIDTH)


def gather_weights(shard):
    whole = lax.all_gather(shard, ("z", "xh", "xl", "c"), axis=0, tiled=False)
    return whole.reshape((4, 2, 2, 2) + shard.shape)


def local(
    tokens,
    lengths,
    attn_gain,
    q_gain,
    key_norm_gain,
    wq_param,
    wq_moment,
    wq_second,
    wq_grad,
    key_weight_matrix,
    key_weight_first_moment,
    key_weight_second_moment,
    key_weight_gradient,
    value_weight_matrix,
    value_weight_first_moment,
    value_weight_second_moment,
    value_weight_gradient,
    wo_param,
    wo_moment,
    wo_second,
    wo_grad,
):
    y, core, xl = lax.axis_index("y"), lax.axis_index("c"), lax.axis_index("xl")
    normed_own = root_mean_scale(tokens.astype(F32), attn_gain).astype(BF16)
    new_k = adamw_step(
        key_weight_matrix, key_weight_first_moment, key_weight_second_moment, key_weight_gradient
    )
    new_v = adamw_step(
        value_weight_matrix,
        value_weight_first_moment,
        value_weight_second_moment,
        value_weight_gradient,
    )
    new_q = adamw_step(wq_param, wq_moment, wq_second, wq_grad)
    new_o = adamw_step(wo_param, wo_moment, wo_second, wo_grad)
    shard_qkv = jnp.concatenate([new_q[0], new_k[0], new_v[0]], axis=1).astype(BF16)
    shard_o = new_o[0].astype(BF16)
    whole_qkv = gather_weights(shard_qkv)
    whole_o = gather_weights(shard_o)
    normed = gather_tokens(normed_own, y, core)
    cosine, sine = position_tables(xl)
    queries, own_kv = qkv_project(
        normed, whole_qkv, cosine, sine, q_gain[None], key_norm_gain[None]
    )
    far_kv = swap_xl(own_kv)
    info = jnp.stack([lengths[0], xl.astype(jnp.int32)])
    context = attend(info, queries, own_kv, far_kv)
    halves = [
        scatter_sum(out_project(context, whole_o, first, 2), y, core) for first in (0, 2)
    ]
    attended = jnp.concatenate(halves, axis=1)
    return (attended,) + new_q + new_k + new_v + new_o


def solution(mesh):
    fine = Mesh(mesh.devices.reshape([SIZES[a] for a in AXES]), AXES)
    dp, tensor = ("z", "xh", "c"), ("y", "xl")
    weight = P(dp, tensor)
    rows = P(dp + tensor, None)
    return jax.shard_map(
        local,
        mesh=fine,
        in_specs=(rows, P(dp), P(), P(), P()) + (weight,) * 16,
        out_specs=(rows,) + (weight,) * 12,
        check_vma=False,
    )
```

time: 713 us -> 282 us (0.40)
  waiting for transfers between devices: 572 us -> 143 us
  matrix products: 88.3 us -> 0 us
  Pallas kernels: 0 us -> 79.6 us
  starting transfers between devices: 0.42 us -> 19.5 us
  other arithmetic: 25.9 us -> 14.5 us
    all_gather x5 -> x2, waiting for transfers between devices: 366 us -> 48.3 us  [gather_weights(): whole = lax.all_gather(shard, ('z', 'xh', 'xl', 'c'), axis=0, tiled=False)]
    reduce_scatter x1 -> x0, waiting for transfers between devices: 206 us -> none  [local(): lax.psum_scatter(rounded, 'tensor', scatter_dimension=0, tiled=True)]
    ppermute x0 -> x10, waiting for transfers between devices: none -> 93.7 us  [permute(): return lambda v: lax.ppermute(v, axes, pairs)]
    pallas_call x0 -> x4, Pallas kernels: none -> 79.6 us  [the longest x1 37.8 us: qkv_project(): pl.pallas_call(qkv_kernel, grid=(2, 4), in_specs=[pl.BlockSpec((OWN, 1280...]
    dot_general x4 -> x0, matrix products: 67 us -> none  [the longest x1 23.5 us: one_group(): jnp.einsum('gst,td->gsd', probs, v_block, preferred_element_type=jnp.floa...]
    sub x1 -> x0, matrix products: 21.3 us -> none  [one_group(): exps = jnp.where(visible[None], jnp.exp(masked - maxima), 0.0)]
    ppermute x0 -> x10, starting transfers between devices: none -> 19.4 us  [permute(): return lambda v: lax.ppermute(v, axes, pairs)]
    convert_element_type x5 -> x7, other arithmetic: 16.5 us -> 1 us  [the longest x6 0.93 us: scatter_sum(): moving = (arrived.astype(F32) + own(s + 1).astype(F32)).astype(BF16)]
  transfers between devices with their start and end apart: 6 -> 12, of which waited for: 5 -> 11; matrix products, arithmetic and copies ran while one was open for 15% -> 3% of each run, Pallas kernels for 0% -> 24%
where the time goes in v1:
time: 282 us
  waiting for transfers between devices  143 us (51%)
  Pallas kernels  79.6 us (28%)
  starting transfers between devices  19.5 us (7%)
  between operations  14.9 us (5%)
  other arithmetic  14.5 us (5%)
  local copies, waits for them, and re-layouts  10.7 us (4%)
    ppermute x10, waiting for transfers between devices, permute(): return lambda v: lax.ppermute(v, axes, pairs)  93.7 us
    all_gather x2, waiting for transfers between devices, gather_weights(): whole = lax.all_gather(shard, ('z', 'xh', 'xl', 'c'), axis=0, tiled=False)  48.3 us
    pallas_call x1, Pallas kernels, qkv_project(): pl.pallas_call(qkv_kernel, grid=(2, 4), in_specs=[pl.BlockSpec((OWN, 1280...  37.8 us
    pallas_call x2, Pallas kernels, out_project(): pl.pallas_call(out_kernel, grid=(count,), in_specs=[pl.BlockSpec((2, OWN,...  23.5 us
    ppermute x10, starting transfers between devices, permute(): return lambda v: lax.ppermute(v, axes, pairs)  19.4 us
    pallas_call x1, Pallas kernels, attend(): pl.pallas_call(attend_kernel, grid=(2, 4), in_specs=[pl.BlockSpec(memory_...  18.2 us
    concatenate x3, other arithmetic, local(): jnp.concatenate([new_q[0], new_k[0], new_v[0]], axis=1).astype(BF16)  10.3 us
  transfers between devices with their start and end apart: 12, of which 11 were waited for; matrix products, arithmetic and copies ran while one was open for 3% of the time, Pallas kernels for 24%

profile of v1, /device:TPU:1, one launch (start us, length us, event | category | flops | bytes accessed | tf_op | source)
XLA Modules:
  0.0 281.9 jit_solution(11230613539909618259)
XLA Ops:
  7.2 2.6 convert_bitcast_fusion.1
  9.8 6.7 %convert_bitcast_fusion = (bf16[1,320,1024]{2,1,0:T(8,128)(2,1)S(1)}, f32[320,1024]{1,0:T(8,128)}, f32[320,1024]{1,0:T(8,128)}, f32[320,1024]{1,0:T(8,128)}, bf1...) fusion(f32[320,1024]{1,0:T(8,128)S(1)} %copy-done.6, ...), kind=kLoop, calls=%fused_computation.33 | loop fusion | flops 10485760 | bytes 19660800 | tf_op jit(solution)/shard_map/concatenate | solution.py:308
  19.9 2.2 copy-done.5
  22.1 3.6 %collective-permute-start = (bf16[128,5120]{1,0:T(8,128)(2,1)S(1)}, bf16[128,5120]{1,0:T(8,128)(2,1)S(1)}, u32[]{:S(2)}, u32[]{:S(2)}) collective-permute-start(bf16[128,5120]{1,0:T(8,128)(2,1)S(1)} %get-tuple-element.34), channel_id=1, source_target_pairs={{0,2},{2,4},{4,6},{6,0},{8,14},{10,8},{12,10},{14,12},{1,3},{3,5},... | collective-permute-start | bytes 3932168 | tf_op jit(solution)/shard_map/ppermute | solution.py:57
  25.6 14.6 %collective-permute-done = bf16[128,5120]{1,0:T(8,128)(2,1)S(1)} collective-permute-done((bf16[128,5120]{1,0:T(8,128)(2,1)S(1)}, bf16[128,5120]{1,0:T(8,128)(2,1)S(1)}, u32[]{:S(2)}, u32[]{:S(2)}) %collective-permute-start) | collective-permute-done | bytes 1310752 | tf_op jit(solution)/shard_map/ppermute | solution.py:57
  40.2 3.2 %collective-permute-start.1 = (bf16[128,5120]{1,0:T(8,128)(2,1)S(1)}, bf16[128,5120]{1,0:T(8,128)(2,1)}, u32[]{:S(2)}, u32[]{:S(2)}) collective-permute-start(bf16[128,5120]{1,0:T(8,128)(2,1)S(1)} %collective-permute-done), channel_id=1, source_target_pairs={{0,2},{2,4},{4,6},{6,0},{8,14},{10,8},{12,10},{14,12},{1,3},{3,5},... | collective-permute-start | bytes 3932168 | tf_op jit(solution)/shard_map/ppermute | solution.py:57
  44.7 13.2 %collective-permute-done.1 = bf16[128,5120]{1,0:T(8,128)(2,1)} collective-permute-done((bf16[128,5120]{1,0:T(8,128)(2,1)S(1)}, bf16[128,5120]{1,0:T(8,128)(2,1)}, u32[]{:S(2)}, u32[]{:S(2)}) %collective-permute-start.1) | collective-permute-done | bytes 1310752 | tf_op jit(solution)/shard_map/ppermute | solution.py:57
  57.9 3.2 %collective-permute-start.2 = (bf16[128,5120]{1,0:T(8,128)(2,1)}, bf16[128,5120]{1,0:T(8,128)(2,1)S(1)}, u32[]{:S(2)}, u32[]{:S(2)}) collective-permute-start(bf16[128,5120]{1,0:T(8,128)(2,1)} %collective-permute-done.1), channel_id=1, source_target_pairs={{0,2},{2,4},{4,6},{6,0},{8,14},{10,8},{12,10},{14,12},{1,3},{3,5},... | collective-permute-start | bytes 3932168 | tf_op jit(solution)/shard_map/ppermute | solution.py:57
  61.2 1.2 bitcast_dynamic-update-slice_fusion.2
  62.3 2.5 bitcast_dynamic-update-slice_fusion.1
  64.8 11.2 %collective-permute-done.2 = bf16[128,5120]{1,0:T(8,128)(2,1)S(1)} collective-permute-done((bf16[128,5120]{1,0:T(8,128)(2,1)}, bf16[128,5120]{1,0:T(8,128)(2,1)S(1)}, u32[]{:S(2)}, u32[]{:S(2)}) %collective-permute-start.2) | collective-permute-done | bytes 1310752 | tf_op jit(solution)/shard_map/ppermute | solution.py:57
  76.0 1.1 bitcast_dynamic-update-slice_fusion
  77.2 39.0 %all-gather.4.cloned.1.call-done = bf16[32,320,1280]{2,1,0:T(8,128)(2,1)} async-done(((bf16[1,320,1280]{2,1,0:T(8,128)(2,1)}), bf16[32,320,1280]{2,1,0:T(8,128)(2,1)}) %all-gather.4.cloned.1.call-update) | async-done | bytes 26214416 | tf_op jit(solution)/shard_map/all_gather | solution.py:268
  116.2 37.8 %qkv.1 = (bf16[2,512,1024]{2,1,0:T(8,128)(2,1)S(1)}, bf16[2,512,256]{2,1,0:T(8,128)(2,1)S(1)}) custom-call(bf16[512,5120]{1,0:T(8,128)(2,1)} %bitcast.58, bf16[4,2,2,2,320,1280]{5,4,3,2,1,0:T(8,128)(2,1)} %bitcast.59, f32[512,128]{1,0:T(8,128)S(1)} %get-tuple-element.42.cos_ref, f32[512,128]{1,0:T(8,128)S(1)} %get-tuple-element.43.sin_ref, ...), custom_call_target="tpu_custom_call" | custom-call | flops 13421772800 | bytes 41943040 | tf_op jit(solution)/shard_map/qkv/pallas_call | solution.py:131
  154.0 1.3 copy-done.2
  155.4 1.1 collective-permute-start.3
  157.2 23.1 %collective-permute-done.3.far_ref = bf16[2,512,256]{2,1,0:T(8,128)(2,1)S(1)} collective-permute-done((bf16[2,512,256]{2,1,0:T(8,128)(2,1)S(1)}, bf16[2,512,256]{2,1,0:T(8,128)(2,1)S(1)}, u32[]{:S(2)}, u32[]{:S(2)}) %collective-permute-start.3) | collective-permute-done | bytes 524320 | tf_op jit(solution)/shard_map/ppermute | solution.py:57
  180.4 1.6 copy-done.3
  182.0 18.2 %attend.1.ctx_ref = bf16[2,512,1024]{2,1,0:T(8,128)(2,1)S(1)} custom-call(s32[2]{0:T(128)S(1)} %pad_add_fusion.info_ref, bf16[2,512,1024]{2,1,0:T(8,128)(2,1)S(1)} %copy-done.3, bf16[2,512,256]{2,1,0:T(8,128)(2,1)S(1)} %get-tuple-element.16.own_ref, bf16[2,512,256]{2,1,0:T(8,128)(2,1)S(1)} %collective-permute-done.3.far_ref), custom_call_target="tpu_custom_call" | custom-call | flops 6442450944 | bytes 5242880 | tf_op jit(solution)/shard_map/attend/pallas_call | solution.py:193
  200.2 9.2 %all-gather.6.cloned.1.call-done = bf16[10240,1024]{1,0:T(8,128)(2,1)} async-done(((bf16[320,1024]{1,0:T(8,128)(2,1)}), bf16[10240,1024]{1,0:T(8,128)(2,1)}) %all-gather.6.cloned.1.call-update) | async-done | bytes 20971536 | tf_op jit(solution)/shard_map/all_gather | solution.py:268
  209.4 11.8 %out_project.2 = bf16[512,2560]{1,0:T(8,128)(2,1)S(1)} custom-call(bf16[2,512,1024]{2,1,0:T(8,128)(2,1)S(1)} %attend.1.ctx_ref, bf16[4,2,2,2,320,1024]{5,4,3,2,1,0:T(8,128)(2,1)} %bitcast.56), custom_call_target="tpu_custom_call" | custom-call | flops 5368709120 | bytes 14680064 | tf_op jit(solution)/shard_map/out_project/pallas_call | solution.py:225
  221.2 2.8 collective-permute-start.4
  224.0 11.8 %out_project.3 = bf16[512,2560]{1,0:T(8,128)(2,1)S(1)} custom-call(bf16[2,512,1024]{2,1,0:T(8,128)(2,1)S(1)} %attend.1.ctx_ref, bf16[4,2,2,2,320,1024]{5,4,3,2,1,0:T(8,128)(2,1)} %bitcast.57), custom_call_target="tpu_custom_call" | custom-call | flops 5368709120 | bytes 14680064 | tf_op jit(solution)/shard_map/out_project/pallas_call | solution.py:225
  237.0 8.7 %collective-permute-done.7 = bf16[128,2560]{1,0:T(8,128)(2,1)S(1)} collective-permute-done((bf16[128,2560]{1,0:T(8,128)(2,1)S(1)}, bf16[128,2560]{1,0:T(8,128)(2,1)S(1)}, u32[]{:S(2)}, u32[]{:S(2)}) %collective-permute-start.7) | collective-permute-done | bytes 655392 | tf_op jit(solution)/shard_map/ppermute | solution.py:57
  245.8 1.5 collective-permute-start.8
  247.3 5.3 %collective-permute-done.5 = bf16[128,2560]{1,0:T(8,128)(2,1)S(1)} collective-permute-done((bf16[128,2560]{1,0:T(8,128)(2,1)S(1)}, bf16[128,2560]{1,0:T(8,128)(2,1)S(1)}, u32[]{:S(2)}, u32[]{:S(2)}) %collective-permute-start.5) | collective-permute-done | bytes 655392 | tf_op jit(solution)/shard_map/ppermute | solution.py:57
  252.8 1.5 collective-permute-start.6
  254.4 5.3 %collective-permute-done.8 = bf16[128,2560]{1,0:T(8,128)(2,1)S(1)} collective-permute-done((bf16[128,2560]{1,0:T(8,128)(2,1)S(1)}, bf16[128,2560]{1,0:T(8,128)(2,1)S(1)}, u32[]{:S(2)}, u32[]{:S(2)}) %collective-permute-start.8) | collective-permute-done | bytes 655392 | tf_op jit(solution)/shard_map/ppermute | solution.py:57
  259.8 1.5 collective-permute-start.9
  261.4 5.3 %collective-permute-done.6 = bf16[128,2560]{1,0:T(8,128)(2,1)S(1)} collective-permute-done((bf16[128,2560]{1,0:T(8,128)(2,1)S(1)}, bf16[128,2560]{1,0:T(8,128)(2,1)S(1)}, u32[]{:S(2)}, u32[]{:S(2)}) %collective-permute-start.6) | collective-permute-done | bytes 655392 | tf_op jit(solution)/shard_map/ppermute | solution.py:57
  266.9 6.9 %collective-permute-done.9 = bf16[128,2560]{1,0:T(8,128)(2,1)S(1)} collective-permute-done((bf16[128,2560]{1,0:T(8,128)(2,1)S(1)}, bf16[128,2560]{1,0:T(8,128)(2,1)S(1)}, u32[]{:S(2)}, u32[]{:S(2)}) %collective-permute-start.9) | collective-permute-done | bytes 655392 | tf_op jit(solution)/shard_map/ppermute | solution.py:57
  273.9 1.2 pad_maximum_fusion
  (39 shorter events, 6.6 us)
Async XLA Ops:
  7.2 2.6 copy-start.6
  7.2 109.0 %all-gather.4.cloned.1.call-start = ((), (), s32[]{:S(2)}) async-start(), calls=%async_computation | async-start | bytes 27033600 | tf_op jit(solution)/shard_map/all_gather | solution.py:268
  16.6 1.8 copy-start.4
  17.5 191.9 %all-gather.6.cloned.1.call-start = ((), (), s32[]{:S(2)}) async-start(), calls=%async_computation.1 | async-start | bytes 21626880 | tf_op jit(solution)/shard_map/all_gather | solution.py:268
  18.7 0.7 copy-start.7
  19.9 2.2 copy-start.5
  22.1 18.1 %collective-permute-start = (bf16[128,5120]{1,0:T(8,128)(2,1)S(1)}, bf16[128,5120]{1,0:T(8,128)(2,1)S(1)}, u32[]{:S(2)}, u32[]{:S(2)}) collective-permute-start(bf16[128,5120]{1,0:T(8,128)(2,1)S(1)} %get-tuple-element.34), channel_id=1, source_target_pairs={{0,2},{2,4},{4,6},{6,0},{8,14},{10,8},{12,10},{14,12},{1,3},{3,5},... | collective-permute-start | bytes 3932168 | tf_op jit(solution)/shard_map/ppermute | solution.py:57
  40.2 17.7 %collective-permute-start.1 = (bf16[128,5120]{1,0:T(8,128)(2,1)S(1)}, bf16[128,5120]{1,0:T(8,128)(2,1)}, u32[]{:S(2)}, u32[]{:S(2)}) collective-permute-start(bf16[128,5120]{1,0:T(8,128)(2,1)S(1)} %collective-permute-done), channel_id=1, source_target_pairs={{0,2},{2,4},{4,6},{6,0},{8,14},{10,8},{12,10},{14,12},{1,3},{3,5},... | collective-permute-start | bytes 3932168 | tf_op jit(solution)/shard_map/ppermute | solution.py:57
  57.9 18.1 %collective-permute-start.2 = (bf16[128,5120]{1,0:T(8,128)(2,1)}, bf16[128,5120]{1,0:T(8,128)(2,1)S(1)}, u32[]{:S(2)}, u32[]{:S(2)}) collective-permute-start(bf16[128,5120]{1,0:T(8,128)(2,1)} %collective-permute-done.1), channel_id=1, source_target_pairs={{0,2},{2,4},{4,6},{6,0},{8,14},{10,8},{12,10},{14,12},{1,3},{3,5},... | collective-permute-start | bytes 3932168 | tf_op jit(solution)/shard_map/ppermute | solution.py:57
  64.8 51.4 %copy-start = (f32[128]{0:T(128)S(1)}, f32[128]{0:T(128)}, u32[]{:S(2)}) copy-start(f32[128]{0:T(128)} %param.24) | copy-start | bytes 1540
  64.8 51.4 %copy-start.1 = (f32[128]{0:T(128)S(1)}, f32[128]{0:T(128)}, u32[]{:S(2)}) copy-start(f32[128]{0:T(128)} %param.25) | copy-start | bytes 1540
  154.0 1.3 copy-start.2
  155.4 25.0 %collective-permute-start.3 = (bf16[2,512,256]{2,1,0:T(8,128)(2,1)S(1)}, bf16[2,512,256]{2,1,0:T(8,128)(2,1)S(1)}, u32[]{:S(2)}, u32[]{:S(2)}) collective-permute-start(bf16[2,512,256]{2,1,0:T(8,128)(2,1)S(1)} %get-tuple-element.16.own_ref), channel_id=1, source_target_pairs={{0,1},{1,0},{2,3},{3,2},{4,5},{5,4},{6,7},{7,6},{8,9},{9,8},{10,11... | collective-permute-start | bytes 1572872 | tf_op jit(solution)/shard_map/ppermute | solution.py:57
  180.4 1.6 copy-start.3
  221.2 15.2 %collective-permute-start.4 = (bf16[128,2560]{1,0:T(8,128)(2,1)S(1)}, bf16[128,2560]{1,0:T(8,128)(2,1)S(1)}, u32[]{:S(2)}, u32[]{:S(2)}) collective-permute-start(bf16[128,2560]{1,0:T(8,128)(2,1)S(1)} %dynamic-slice_bitcast_fusion.1), channel_id=1, source_target_pairs={{0,2},{2,4},{4,6},{6,0},{8,14},{10,8},{12,10},{14,12},{1,3},{3,5},... | collective-permute-start | bytes 1966088 | tf_op jit(solution)/shard_map/ppermute | solution.py:57
  235.8 9.8 %collective-permute-start.7 = (bf16[128,2560]{1,0:T(8,128)(2,1)S(1)}, bf16[128,2560]{1,0:T(8,128)(2,1)S(1)}, u32[]{:S(2)}, u32[]{:S(2)}) collective-permute-start(bf16[128,2560]{1,0:T(8,128)(2,1)S(1)} %dynamic-slice_bitcast_fusion), channel_id=1, source_target_pairs={{0,2},{2,4},{4,6},{6,0},{8,14},{10,8},{12,10},{14,12},{1,3},{3,5},... | collective-permute-start | bytes 1966088 | tf_op jit(solution)/shard_map/ppermute | solution.py:57
  236.6 16.0 %collective-permute-start.5 = (bf16[128,2560]{1,0:T(8,128)(2,1)S(1)}, bf16[128,2560]{1,0:T(8,128)(2,1)S(1)}, u32[]{:S(2)}, u32[]{:S(2)}) collective-permute-start(bf16[128,2560]{1,0:T(8,128)(2,1)S(1)} %fusion.10), channel_id=1, source_target_pairs={{0,2},{2,4},{4,6},{6,0},{8,14},{10,8},{12,10},{14,12},{1,3},{3,5},... | collective-permute-start | bytes 1966088 | tf_op jit(solution)/shard_map/ppermute | solution.py:57
  245.8 13.9 %collective-permute-start.8 = (bf16[128,2560]{1,0:T(8,128)(2,1)S(1)}, bf16[128,2560]{1,0:T(8,128)(2,1)S(1)}, u32[]{:S(2)}, u32[]{:S(2)}) collective-permute-start(bf16[128,2560]{1,0:T(8,128)(2,1)S(1)} %fusion.7), channel_id=1, source_target_pairs={{0,2},{2,4},{4,6},{6,0},{8,14},{10,8},{12,10},{14,12},{1,3},{3,5},... | collective-permute-start | bytes 1966088 | tf_op jit(solution)/shard_map/ppermute | solution.py:57
  252.8 13.9 %collective-permute-start.6 = (bf16[128,2560]{1,0:T(8,128)(2,1)S(1)}, bf16[128,2560]{1,0:T(8,128)(2,1)S(1)}, u32[]{:S(2)}, u32[]{:S(2)}) collective-permute-start(bf16[128,2560]{1,0:T(8,128)(2,1)S(1)} %fusion.9), channel_id=1, source_target_pairs={{0,2},{2,4},{4,6},{6,0},{8,14},{10,8},{12,10},{14,12},{1,3},{3,5},... | collective-permute-start | bytes 1966088 | tf_op jit(solution)/shard_map/ppermute | solution.py:57
  259.8 13.9 %collective-permute-start.9 = (bf16[128,2560]{1,0:T(8,128)(2,1)S(1)}, bf16[128,2560]{1,0:T(8,128)(2,1)S(1)}, u32[]{:S(2)}, u32[]{:S(2)}) collective-permute-start(bf16[128,2560]{1,0:T(8,128)(2,1)S(1)} %fusion.6), channel_id=1, source_target_pairs={{0,2},{2,4},{4,6},{6,0},{8,14},{10,8},{12,10},{14,12},{1,3},{3,5},... | collective-permute-start | bytes 1966088 | tf_op jit(solution)/shard_map/ppermute | solution.py:57
Sparse Core Ops, SparseCore 0:
  17.7 98.4 all-gather.3
  118.5 90.9 all-gather.5

commit v2 on v1

--- a/solution.py
+++ b/solution.py
@@ -165,6 +165,7 @@
         n = (j + 1) * BLOCK
         keys = jnp.concatenate([own_ref[0, :n, :128], far_ref[0, :n, :128]], axis=0)
         values = jnp.concatenate([own_ref[0, :n, 128:], far_ref[0, :n, 128:]], axis=0)
+        values = jnp.concatenate([values, jnp.ones_like(values)], axis=1)
         row = lax.broadcasted_iota(jnp.int32, (BLOCK, 2 * n), 0)
         col = lax.broadcasted_iota(jnp.int32, (BLOCK, 2 * n), 1)
         own = col < n
@@ -180,10 +181,9 @@
             )
             scores = scores + bias
             top = jnp.max(scores, axis=-1, keepdims=True)
-            exps = jnp.exp2((scores - top) * SCALE)
-            total = jnp.sum(exps, axis=-1, keepdims=True)
-            mixed = jnp.dot(exps.astype(BF16), values, preferred_element_type=F32)
-            o_ref[0, :, lanes] = (mixed / total).astype(BF16)
+            exps = jnp.exp2((scores - top) * SCALE).astype(BF16)
+            mixed = jnp.dot(exps, values, preferred_element_type=F32)
+            o_ref[0, :, lanes] = (mixed[:, :128] / mixed[:, 128:]).astype(BF16)
 
     for j in range(4):
         pl.when(block == j)(functools.partial(body, j))
@@ -262,6 +262,10 @@
         if s < 3:
             moving = ring_y(moving)
     return whole.reshape(OWN, WIDTH)
+
+
+def after(value, *before):
+    return lax.optimization_barrier((value,) + before)[0]
 
 
 def gather_weights(shard):
@@ -293,7 +297,6 @@
     wo_grad,
 ):
     y, core, xl = lax.axis_index("y"), lax.axis_index("c"), lax.axis_index("xl")
-    normed_own = root_mean_scale(tokens.astype(F32), attn_gain).astype(BF16)
     new_k = adamw_step(
         key_weight_matrix, key_weight_first_moment, key_weight_second_moment, key_weight_gradient
     )
@@ -304,10 +307,12 @@
         value_weight_gradient,
     )
     new_q = adamw_step(wq_param, wq_moment, wq_second, wq_grad)
+    shard_qkv = jnp.concatenate([new_q[0], new_k[0], new_v[0]], axis=1).astype(BF16)
+    whole_qkv = gather_weights(shard_qkv)
+    wo_grad, tokens = after((wo_grad, tokens), shard_qkv)
     new_o = adamw_step(wo_param, wo_moment, wo_second, wo_grad)
-    shard_qkv = jnp.concatenate([new_q[0], new_k[0], new_v[0]], axis=1).astype(BF16)
     shard_o = new_o[0].astype(BF16)
-    whole_qkv = gather_weights(shard_qkv)
+    normed_own = root_mean_scale(tokens.astype(F32), attn_gain).astype(BF16)
     whole_o = gather_weights(shard_o)
     normed = gather_tokens(normed_own, y, core)
     cosine, sine = position_tables(xl)
@@ -318,7 +323,8 @@
     info = jnp.stack([lengths[0], xl.astype(jnp.int32)])
     context = attend(info, queries, own_kv, far_kv)
     halves = [
-        scatter_sum(out_project(context, whole_o, first, 2), y, core) for first in (0, 2)
+        scatter_sum(out_project(context, whole_o, first, count), y, core)
+        for first, count in ((0, 2), (2, 2))
     ]
     attended = jnp.concatenate(halves, axis=1)
     return (attended,) + new_q + new_k + new_v + new_o

time: 282 us -> 280 us (level)
  Pallas kernels: 79.6 us -> 71.8 us
    pallas_call x1, Pallas kernels: 18.2 us -> 10.4 us  [attend(): pl.pallas_call(attend_kernel, grid=(2, 4), in_specs=[pl.BlockSpec(memory_...]
    convert_element_type x0 -> x1, other arithmetic: none -> 5.21 us  [local(): shard_o = new_o[0].astype(BF16)]
    unnamed x16 -> x32, local copies, waits for them, and re-layouts: 5.26 us -> 5.9 us
  transfers between devices with their start and end apart: 12 -> 12, of which waited for: 11 -> 11; matrix products, arithmetic and copies ran while one was open for 3% -> 5% of each run, Pallas kernels for 24% -> 21%
where the time goes in v2:
time: 280 us; the launch traced here: 279 us
  waiting for transfers between devices  144 us (51%)
  Pallas kernels  71.8 us (26%)
  starting transfers between devices  20.1 us (7%)
  other arithmetic  17 us (6%)
  between operations  15 us (5%)
  local copies, waits for them, and re-layouts  11.4 us (4%)
    ppermute x10, waiting for transfers between devices, permute(): return lambda v: lax.ppermute(v, axes, pairs)  93.7 us
    all_gather x2, waiting for transfers between devices, gather_weights(): whole = lax.all_gather(shard, ('z', 'xh', 'xl', 'c'), axis=0, tiled=False)  50.2 us
    pallas_call x1, Pallas kernels, qkv_project(): pl.pallas_call(qkv_kernel, grid=(2, 4), in_specs=[pl.BlockSpec((OWN, 1280...  37.8 us
    pallas_call x2, Pallas kernels, out_project(): pl.pallas_call(out_kernel, grid=(count,), in_specs=[pl.BlockSpec((2, OWN,...  23.5 us
    ppermute x10, starting transfers between devices, permute(): return lambda v: lax.ppermute(v, axes, pairs)  20.1 us
    pallas_call x1, Pallas kernels, attend(): pl.pallas_call(attend_kernel, grid=(2, 4), in_specs=[pl.BlockSpec(memory_...  10.4 us
    concatenate x3, other arithmetic, local(): jnp.concatenate([new_q[0], new_k[0], new_v[0]], axis=1).astype(BF16)  7.53 us
    unnamed x32, local copies, waits for them, and re-layouts  5.9 us
  transfers between devices with their start and end apart: 12, of which 11 were waited for; matrix products, arithmetic and copies ran while one was open for 5% of the time, Pallas kernels for 21%

profile of v2, /device:TPU:1, one launch (start us, length us, event | category | flops | bytes accessed | tf_op | source)
XLA Modules:
  0.0 279.2 jit_solution(8170219475309429813)
XLA Ops:
  7.3 5.5 %convert_bitcast_fusion = (bf16[1,320,1024]{2,1,0:T(8,128)(2,1)S(1)}, f32[320,1024]{1,0:T(8,128)}, f32[320,1024]{1,0:T(8,128)}, f32[320,1024]{1,0:T(8,128)}) fusion(f32[320,1024]{1,0:T(8,128)} %param.26, f32[320,1024]{1,0:T(8,128)} %param.29, f32[320,1024]{1,0:T(8,128)} %param.27, f32[320,1024]{1,0:T(8,128)} %param.28), kind=kLoop, calls=%fused_computation.33 | loop fusion | flops 5242880 | bytes 9830400 | tf_op jit(solution)/shard_map/concatenate | solution.py:310
  15.6 5.2 %fusion.14 = (bf16[320,1024]{1,0:T(8,128)(2,1)}, f32[320,1024]{1,0:T(8,128)}, f32[320,1024]{1,0:T(8,128)}, f32[320,1024]{1,0:T(8,128)}) fusion(f32[320,1024]{1,0:T(8,128)S(1)} %copy-done.6, f32[320,1024]{1,0:T(8,128)} %param.41, f32[320,1024]{1,0:T(8,128)} %param.39, f32[320,1024]{1,0:T(8,128)} %param.40), kind=kLoop, calls=%fused_computation.54 | loop fusion | flops 5242880 | bytes 9830400 | tf_op jit(solution)/shard_map/convert_element_type | solution.py:314
  22.4 2.2 copy-done.5
  24.6 3.6 %collective-permute-start = (bf16[128,5120]{1,0:T(8,128)(2,1)S(1)}, bf16[128,5120]{1,0:T(8,128)(2,1)S(1)}, u32[]{:S(2)}, u32[]{:S(2)}) collective-permute-start(bf16[128,5120]{1,0:T(8,128)(2,1)S(1)} %get-tuple-element.38), channel_id=1, source_target_pairs={{0,2},{2,4},{4,6},{6,0},{8,14},{10,8},{12,10},{14,12},{1,3},{3,5},... | collective-permute-start | bytes 3932168 | tf_op jit(solution)/shard_map/ppermute | solution.py:57
  28.2 14.6 %collective-permute-done = bf16[128,5120]{1,0:T(8,128)(2,1)S(1)} collective-permute-done((bf16[128,5120]{1,0:T(8,128)(2,1)S(1)}, bf16[128,5120]{1,0:T(8,128)(2,1)S(1)}, u32[]{:S(2)}, u32[]{:S(2)}) %collective-permute-start) | collective-permute-done | bytes 1310752 | tf_op jit(solution)/shard_map/ppermute | solution.py:57
  42.7 3.5 %collective-permute-start.1 = (bf16[128,5120]{1,0:T(8,128)(2,1)S(1)}, bf16[128,5120]{1,0:T(8,128)(2,1)}, u32[]{:S(2)}, u32[]{:S(2)}) collective-permute-start(bf16[128,5120]{1,0:T(8,128)(2,1)S(1)} %collective-permute-done), channel_id=1, source_target_pairs={{0,2},{2,4},{4,6},{6,0},{8,14},{10,8},{12,10},{14,12},{1,3},{3,5},... | collective-permute-start | bytes 3932168 | tf_op jit(solution)/shard_map/ppermute | solution.py:57
  47.5 13.2 %collective-permute-done.1 = bf16[128,5120]{1,0:T(8,128)(2,1)} collective-permute-done((bf16[128,5120]{1,0:T(8,128)(2,1)S(1)}, bf16[128,5120]{1,0:T(8,128)(2,1)}, u32[]{:S(2)}, u32[]{:S(2)}) %collective-permute-start.1) | collective-permute-done | bytes 1310752 | tf_op jit(solution)/shard_map/ppermute | solution.py:57
  60.8 3.5 %collective-permute-start.2 = (bf16[128,5120]{1,0:T(8,128)(2,1)}, bf16[128,5120]{1,0:T(8,128)(2,1)S(1)}, u32[]{:S(2)}, u32[]{:S(2)}) collective-permute-start(bf16[128,5120]{1,0:T(8,128)(2,1)} %collective-permute-done.1), channel_id=1, source_target_pairs={{0,2},{2,4},{4,6},{6,0},{8,14},{10,8},{12,10},{14,12},{1,3},{3,5},... | collective-permute-start | bytes 3932168 | tf_op jit(solution)/shard_map/ppermute | solution.py:57
  64.3 1.1 bitcast_dynamic-update-slice_fusion.2
  65.5 2.5 bitcast_dynamic-update-slice_fusion.1
  67.9 11.2 %collective-permute-done.2 = bf16[128,5120]{1,0:T(8,128)(2,1)S(1)} collective-permute-done((bf16[128,5120]{1,0:T(8,128)(2,1)}, bf16[128,5120]{1,0:T(8,128)(2,1)S(1)}, u32[]{:S(2)}, u32[]{:S(2)}) %collective-permute-start.2) | collective-permute-done | bytes 1310752 | tf_op jit(solution)/shard_map/ppermute | solution.py:57
  79.2 1.1 bitcast_dynamic-update-slice_fusion
  80.3 33.3 %all-gather.4.cloned.1.call-done = bf16[32,320,1280]{2,1,0:T(8,128)(2,1)} async-done(((bf16[1,320,1280]{2,1,0:T(8,128)(2,1)}), bf16[32,320,1280]{2,1,0:T(8,128)(2,1)}) %all-gather.4.cloned.1.call-update) | async-done | bytes 26214416 | tf_op jit(solution)/shard_map/all_gather | solution.py:272
  113.6 37.8 %qkv.1 = (bf16[2,512,1024]{2,1,0:T(8,128)(2,1)S(1)}, bf16[2,512,256]{2,1,0:T(8,128)(2,1)S(1)}) custom-call(bf16[512,5120]{1,0:T(8,128)(2,1)} %bitcast.58, bf16[4,2,2,2,320,1280]{5,4,3,2,1,0:T(8,128)(2,1)} %bitcast.59, f32[512,128]{1,0:T(8,128)S(1)} %get-tuple-element.46.cos_ref, f32[512,128]{1,0:T(8,128)S(1)} %get-tuple-element.47.sin_ref, ...), custom_call_target="tpu_custom_call" | custom-call | flops 13421772800 | bytes 41943040 | tf_op jit(solution)/shard_map/qkv/pallas_call | solution.py:131
  151.4 1.3 copy-done.2
  152.7 1.1 collective-permute-start.3
  154.6 23.1 %collective-permute-done.3.far_ref = bf16[2,512,256]{2,1,0:T(8,128)(2,1)S(1)} collective-permute-done((bf16[2,512,256]{2,1,0:T(8,128)(2,1)S(1)}, bf16[2,512,256]{2,1,0:T(8,128)(2,1)S(1)}, u32[]{:S(2)}, u32[]{:S(2)}) %collective-permute-start.3) | collective-permute-done | bytes 524320 | tf_op jit(solution)/shard_map/ppermute | solution.py:57
  177.8 1.6 copy-done.3
  179.4 10.4 %attend.1.ctx_ref = bf16[2,512,1024]{2,1,0:T(8,128)(2,1)S(1)} custom-call(s32[2]{0:T(128)S(1)} %pad_add_fusion.info_ref, bf16[2,512,1024]{2,1,0:T(8,128)(2,1)S(1)} %copy-done.3, bf16[2,512,256]{2,1,0:T(8,128)(2,1)S(1)} %get-tuple-element.19.own_ref, bf16[2,512,256]{2,1,0:T(8,128)(2,1)S(1)} %collective-permute-done.3.far_ref), custom_call_target="tpu_custom_call" | custom-call | flops 6442450944 | bytes 5242880 | tf_op jit(solution)/shard_map/attend/pallas_call | solution.py:193
  189.8 16.9 %all-gather.6.cloned.1.call-done = bf16[10240,1024]{1,0:T(8,128)(2,1)} async-done(((bf16[320,1024]{1,0:T(8,128)(2,1)}), bf16[10240,1024]{1,0:T(8,128)(2,1)}) %all-gather.6.cloned.1.call-update) | async-done | bytes 20971536 | tf_op jit(solution)/shard_map/all_gather | solution.py:272
  206.7 11.8 %out_project.2 = bf16[512,2560]{1,0:T(8,128)(2,1)S(1)} custom-call(bf16[2,512,1024]{2,1,0:T(8,128)(2,1)S(1)} %attend.1.ctx_ref, bf16[4,2,2,2,320,1024]{5,4,3,2,1,0:T(8,128)(2,1)} %bitcast.56), custom_call_target="tpu_custom_call" | custom-call | flops 5368709120 | bytes 14680064 | tf_op jit(solution)/shard_map/out_project/pallas_call | solution.py:225
  218.6 2.5 collective-permute-start.4
  221.1 11.8 %out_project.3 = bf16[512,2560]{1,0:T(8,128)(2,1)S(1)} custom-call(bf16[2,512,1024]{2,1,0:T(8,128)(2,1)S(1)} %attend.1.ctx_ref, bf16[4,2,2,2,320,1024]{5,4,3,2,1,0:T(8,128)(2,1)} %bitcast.57), custom_call_target="tpu_custom_call" | custom-call | flops 5368709120 | bytes 14680064 | tf_op jit(solution)/shard_map/out_project/pallas_call | solution.py:225
  234.3 8.7 %collective-permute-done.7 = bf16[128,2560]{1,0:T(8,128)(2,1)S(1)} collective-permute-done((bf16[128,2560]{1,0:T(8,128)(2,1)S(1)}, bf16[128,2560]{1,0:T(8,128)(2,1)S(1)}, u32[]{:S(2)}, u32[]{:S(2)}) %collective-permute-start.7) | collective-permute-done | bytes 655392 | tf_op jit(solution)/shard_map/ppermute | solution.py:57
  243.1 1.5 collective-permute-start.8
  244.6 5.3 %collective-permute-done.5 = bf16[128,2560]{1,0:T(8,128)(2,1)S(1)} collective-permute-done((bf16[128,2560]{1,0:T(8,128)(2,1)S(1)}, bf16[128,2560]{1,0:T(8,128)(2,1)S(1)}, u32[]{:S(2)}, u32[]{:S(2)}) %collective-permute-start.5) | collective-permute-done | bytes 655392 | tf_op jit(solution)/shard_map/ppermute | solution.py:57
  250.1 1.5 collective-permute-start.6
  251.7 5.3 %collective-permute-done.8 = bf16[128,2560]{1,0:T(8,128)(2,1)S(1)} collective-permute-done((bf16[128,2560]{1,0:T(8,128)(2,1)S(1)}, bf16[128,2560]{1,0:T(8,128)(2,1)S(1)}, u32[]{:S(2)}, u32[]{:S(2)}) %collective-permute-start.8) | collective-permute-done | bytes 655392 | tf_op jit(solution)/shard_map/ppermute | solution.py:57
  257.1 1.5 collective-permute-start.9
  258.7 5.3 %collective-permute-done.6 = bf16[128,2560]{1,0:T(8,128)(2,1)S(1)} collective-permute-done((bf16[128,2560]{1,0:T(8,128)(2,1)S(1)}, bf16[128,2560]{1,0:T(8,128)(2,1)S(1)}, u32[]{:S(2)}, u32[]{:S(2)}) %collective-permute-start.6) | collective-permute-done | bytes 655392 | tf_op jit(solution)/shard_map/ppermute | solution.py:57
  264.2 6.9 %collective-permute-done.9 = bf16[128,2560]{1,0:T(8,128)(2,1)S(1)} collective-permute-done((bf16[128,2560]{1,0:T(8,128)(2,1)S(1)}, bf16[128,2560]{1,0:T(8,128)(2,1)S(1)}, u32[]{:S(2)}, u32[]{:S(2)}) %collective-permute-start.9) | collective-permute-done | bytes 655392 | tf_op jit(solution)/shard_map/ppermute | solution.py:57
  271.2 1.2 pad_maximum_fusion
  (56 shorter events, 7.9 us)
Async XLA Ops:
  7.2 5.6 %copy-start.11 = (f32[320,128]{1,0:T(8,128)S(1)}, f32[320,128]{1,0:T(8,128)}, u32[]{:S(2)}) copy-start(f32[320,128]{1,0:T(8,128)} %param.30) | copy-start | bytes 491524
  7.2 5.6 %copy-start.14 = (f32[320,128]{1,0:T(8,128)S(1)}, f32[320,128]{1,0:T(8,128)}, u32[]{:S(2)}) copy-start(f32[320,128]{1,0:T(8,128)} %param.31) | copy-start | bytes 491524
  7.2 5.6 %copy-start.13 = (f32[320,128]{1,0:T(8,128)S(1)}, f32[320,128]{1,0:T(8,128)}, u32[]{:S(2)}) copy-start(f32[320,128]{1,0:T(8,128)} %param.32) | copy-start | bytes 491524
  7.2 5.6 %copy-start.12 = (f32[320,128]{1,0:T(8,128)S(1)}, f32[320,128]{1,0:T(8,128)}, u32[]{:S(2)}) copy-start(f32[320,128]{1,0:T(8,128)} %param.33) | copy-start | bytes 491524
  7.2 5.6 %copy-start.7 = (f32[320,128]{1,0:T(8,128)S(1)}, f32[320,128]{1,0:T(8,128)}, u32[]{:S(2)}) copy-start(f32[320,128]{1,0:T(8,128)} %param.34) | copy-start | bytes 491524
  7.2 5.6 %copy-start.9 = (f32[320,128]{1,0:T(8,128)S(1)}, f32[320,128]{1,0:T(8,128)}, u32[]{:S(2)}) copy-start(f32[320,128]{1,0:T(8,128)} %param.35) | copy-start | bytes 491524
  7.2 5.6 %copy-start.10 = (f32[320,128]{1,0:T(8,128)S(1)}, f32[320,128]{1,0:T(8,128)}, u32[]{:S(2)}) copy-start(f32[320,128]{1,0:T(8,128)} %param.36) | copy-start | bytes 491524
  7.3 5.6 %copy-start.8 = (f32[320,128]{1,0:T(8,128)S(1)}, f32[320,128]{1,0:T(8,128)}, u32[]{:S(2)}) copy-start(f32[320,128]{1,0:T(8,128)} %param.37) | copy-start | bytes 491524
  7.3 106.3 %all-gather.4.cloned.1.call-start = ((), (), s32[]{:S(2)}) async-start(), calls=%async_computation | async-start | bytes 27033600 | tf_op jit(solution)/shard_map/all_gather | solution.py:272
  13.9 1.6 copy-start.6
  14.9 191.8 %all-gather.6.cloned.1.call-start = ((), (), s32[]{:S(2)}) async-start(), calls=%async_computation.1 | async-start | bytes 21626880 | tf_op jit(solution)/shard_map/all_gather | solution.py:272
  15.6 5.3 %copy-start.4 = (bf16[128,5120]{1,0:T(8,128)(2,1)S(1)}, bf16[128,5120]{1,0:T(8,128)(2,1)}, u32[]{:S(2)}) copy-start(bf16[128,5120]{1,0:T(8,128)(2,1)} %param.21) | copy-start | bytes 3932164
  21.2 0.7 copy-start.15
  22.4 2.3 copy-start.5
  24.6 18.1 %collective-permute-start = (bf16[128,5120]{1,0:T(8,128)(2,1)S(1)}, bf16[128,5120]{1,0:T(8,128)(2,1)S(1)}, u32[]{:S(2)}, u32[]{:S(2)}) collective-permute-start(bf16[128,5120]{1,0:T(8,128)(2,1)S(1)} %get-tuple-element.38), channel_id=1, source_target_pairs={{0,2},{2,4},{4,6},{6,0},{8,14},{10,8},{12,10},{14,12},{1,3},{3,5},... | collective-permute-start | bytes 3932168 | tf_op jit(solution)/shard_map/ppermute | solution.py:57
  42.7 18.1 %collective-permute-start.1 = (bf16[128,5120]{1,0:T(8,128)(2,1)S(1)}, bf16[128,5120]{1,0:T(8,128)(2,1)}, u32[]{:S(2)}, u32[]{:S(2)}) collective-permute-start(bf16[128,5120]{1,0:T(8,128)(2,1)S(1)} %collective-permute-done), channel_id=1, source_target_pairs={{0,2},{2,4},{4,6},{6,0},{8,14},{10,8},{12,10},{14,12},{1,3},{3,5},... | collective-permute-start | bytes 3932168 | tf_op jit(solution)/shard_map/ppermute | solution.py:57
  60.8 18.4 %collective-permute-start.2 = (bf16[128,5120]{1,0:T(8,128)(2,1)}, bf16[128,5120]{1,0:T(8,128)(2,1)S(1)}, u32[]{:S(2)}, u32[]{:S(2)}) collective-permute-start(bf16[128,5120]{1,0:T(8,128)(2,1)} %collective-permute-done.1), channel_id=1, source_target_pairs={{0,2},{2,4},{4,6},{6,0},{8,14},{10,8},{12,10},{14,12},{1,3},{3,5},... | collective-permute-start | bytes 3932168 | tf_op jit(solution)/shard_map/ppermute | solution.py:57
  67.9 45.7 %copy-start = (f32[128]{0:T(128)S(1)}, f32[128]{0:T(128)}, u32[]{:S(2)}) copy-start(f32[128]{0:T(128)} %param.24) | copy-start | bytes 1540
  67.9 45.7 %copy-start.1 = (f32[128]{0:T(128)S(1)}, f32[128]{0:T(128)}, u32[]{:S(2)}) copy-start(f32[128]{0:T(128)} %param.25) | copy-start | bytes 1540
  151.4 1.3 copy-start.2
  152.7 25.0 %collective-permute-start.3 = (bf16[2,512,256]{2,1,0:T(8,128)(2,1)S(1)}, bf16[2,512,256]{2,1,0:T(8,128)(2,1)S(1)}, u32[]{:S(2)}, u32[]{:S(2)}) collective-permute-start(bf16[2,512,256]{2,1,0:T(8,128)(2,1)S(1)} %get-tuple-element.19.own_ref), channel_id=1, source_target_pairs={{0,1},{1,0},{2,3},{3,2},{4,5},{5,4},{6,7},{7,6},{8,9},{9,8},{10,11... | collective-permute-start | bytes 1572872 | tf_op jit(solution)/shard_map/ppermute | solution.py:57
  177.8 1.6 copy-start.3
  218.6 15.2 %collective-permute-start.4 = (bf16[128,2560]{1,0:T(8,128)(2,1)S(1)}, bf16[128,2560]{1,0:T(8,128)(2,1)S(1)}, u32[]{:S(2)}, u32[]{:S(2)}) collective-permute-start(bf16[128,2560]{1,0:T(8,128)(2,1)S(1)} %dynamic-slice_bitcast_fusion.1), channel_id=1, source_target_pairs={{0,2},{2,4},{4,6},{6,0},{8,14},{10,8},{12,10},{14,12},{1,3},{3,5},... | collective-permute-start | bytes 1966088 | tf_op jit(solution)/shard_map/ppermute | solution.py:57
  232.9 10.0 %collective-permute-start.7 = (bf16[128,2560]{1,0:T(8,128)(2,1)S(1)}, bf16[128,2560]{1,0:T(8,128)(2,1)S(1)}, u32[]{:S(2)}, u32[]{:S(2)}) collective-permute-start(bf16[128,2560]{1,0:T(8,128)(2,1)S(1)} %dynamic-slice_bitcast_fusion), channel_id=1, source_target_pairs={{0,2},{2,4},{4,6},{6,0},{8,14},{10,8},{12,10},{14,12},{1,3},{3,5},... | collective-permute-start | bytes 1966088 | tf_op jit(solution)/shard_map/ppermute | solution.py:57
  233.9 16.0 %collective-permute-start.5 = (bf16[128,2560]{1,0:T(8,128)(2,1)S(1)}, bf16[128,2560]{1,0:T(8,128)(2,1)S(1)}, u32[]{:S(2)}, u32[]{:S(2)}) collective-permute-start(bf16[128,2560]{1,0:T(8,128)(2,1)S(1)} %fusion.10), channel_id=1, source_target_pairs={{0,2},{2,4},{4,6},{6,0},{8,14},{10,8},{12,10},{14,12},{1,3},{3,5},... | collective-permute-start | bytes 1966088 | tf_op jit(solution)/shard_map/ppermute | solution.py:57
  243.1 13.9 %collective-permute-start.8 = (bf16[128,2560]{1,0:T(8,128)(2,1)S(1)}, bf16[128,2560]{1,0:T(8,128)(2,1)S(1)}, u32[]{:S(2)}, u32[]{:S(2)}) collective-permute-start(bf16[128,2560]{1,0:T(8,128)(2,1)S(1)} %fusion.7), channel_id=1, source_target_pairs={{0,2},{2,4},{4,6},{6,0},{8,14},{10,8},{12,10},{14,12},{1,3},{3,5},... | collective-permute-start | bytes 1966088 | tf_op jit(solution)/shard_map/ppermute | solution.py:57
  250.1 13.9 %collective-permute-start.6 = (bf16[128,2560]{1,0:T(8,128)(2,1)S(1)}, bf16[128,2560]{1,0:T(8,128)(2,1)S(1)}, u32[]{:S(2)}, u32[]{:S(2)}) collective-permute-start(bf16[128,2560]{1,0:T(8,128)(2,1)S(1)} %fusion.9), channel_id=1, source_target_pairs={{0,2},{2,4},{4,6},{6,0},{8,14},{10,8},{12,10},{14,12},{1,3},{3,5},... | collective-permute-start | bytes 1966088 | tf_op jit(solution)/shard_map/ppermute | solution.py:57
  257.1 13.9 %collective-permute-start.9 = (bf16[128,2560]{1,0:T(8,128)(2,1)S(1)}, bf16[128,2560]{1,0:T(8,128)(2,1)S(1)}, u32[]{:S(2)}, u32[]{:S(2)}) collective-permute-start(bf16[128,2560]{1,0:T(8,128)(2,1)S(1)} %fusion.6), channel_id=1, source_target_pairs={{0,2},{2,4},{4,6},{6,0},{8,14},{10,8},{12,10},{14,12},{1,3},{3,5},... | collective-permute-start | bytes 1966088 | tf_op jit(solution)/shard_map/ppermute | solution.py:57
Sparse Core Ops, SparseCore 0:
  15.1 98.4 all-gather.3
  115.8 90.8 all-gather.5
